TPU v7x, 256 devices: a whole 4x4x8 slice. The times are simulated.
256 devices in a mesh: src: 16 (over x, z_hi, core), tgt: 16 (over z_lo, y).
Axes of the slice: x: 4, y: 4, z: 8 (z_hi: 2, z_lo: 4; z = z_hi * 4 + z_lo), core: 2. Of those that a mesh axis runs over, the one named last changes fastest.
Arguments:
- weights: float32 [2, 16, 16, 256, 256], P(None, 'src', 'tgt'), may hold values from -0.375 to 0.375
- slowness_terms: float32 [3], replicated, may hold values from 0.05 to 0.25
Outputs:
- final_weights: float32 [2, 16, 16, 256, 256], P(None, 'src', 'tgt')
All inputs are finite; a program needn't handle non-finite values.
Results may differ from a plain program's by a relative error of at most 0.0005.
Values sent between devices are 32-bit elements; how exact they have to be, the bound alone decides.
A program may use at most 64 MiB of HBM per device.

v0:
```python
import math

import jax
import jax.numpy as jnp
import ml_dtypes
import numpy as np
from jax import lax
from jax.experimental import pallas as pl
from jax.experimental.pallas import tpu as pltpu
from jax.sharding import PartitionSpec as P

MESH = pl.DeviceIdType.MESH
NODES = 16
LANES = 128
PERIOD = 2.0 * math.pi


def nodes_np():
    t = np.arange(NODES, dtype=np.float64)
    return 0.5 - 0.5 * np.cos((2.0 * t + 1.0) * math.pi / (2 * NODES))


def merge_matrix(axis):
    z = nodes_np()
    eye = np.eye(NODES)
    blocks = []
    for c in range(2):
        at = (c + z) / 2.0
        lag = np.ones((NODES, NODES))
        for t in range(NODES):
            for m in range(NODES):
                if m != t:
                    lag[:, t] *= (at - z[m]) / (z[t] - z[m])
        if axis == 0:
            full = lag[:, None, :, None] * eye[None, :, None, :]
        else:
            full = eye[:, None, :, None] * lag[None, :, None, :]
        blocks.append(full.reshape(256, 256))
    return np.concatenate(blocks)


def split_matrix(axis):
    full = merge_matrix(axis)
    high = full.astype(np.float32).astype(ml_dtypes.bfloat16)
    low = (full - high.astype(np.float64)).astype(np.float32).astype(ml_dtypes.bfloat16)
    return np.concatenate([high, low, high])


def fit(fn, count):
    u = 0.125 - 0.125 * np.cos((np.arange(400) + 0.5) * math.pi / 400)
    c = np.polynomial.chebyshev.Chebyshev.fit(u, fn(np.sqrt(u)), count - 1, domain=[0, 0.25])
    return [float(v) for v in c.convert(kind=np.polynomial.Polynomial, domain=[-1, 1]).coef]


SIN_FIT = fit(lambda f: np.sin(math.pi * f) / f, 5)
COS_FIT = fit(lambda f: np.cos(math.pi * f), 6)


def horner(u, coef):
    acc = jnp.full_like(u, coef[-1])
    for v in coef[-2::-1]:
        acc = acc * u + v
    return acc


def unit(turns):
    f = turns - jnp.round(turns)
    u = f * f
    s = f * horner(u, SIN_FIT)
    c = horner(u, COS_FIT)
    return 1.0 - 2.0 * s * s, 2.0 * s * c


def own_bits():
    src, tgt = lax.axis_index("src"), lax.axis_index("tgt")
    bits = [lax.rem(src // 2**m, 2) for m in range(4)]
    return bits + [lax.rem(tgt // 2**m, 2) for m in range(4)]


def chip():
    src, tgt = lax.axis_index("src"), lax.axis_index("tgt")
    x, z_hi, core = src // 4, lax.rem(src // 2, 2), lax.rem(src, 2)
    return x, lax.rem(tgt, 4), z_hi * 4 + tgt // 4, core


def device_of(x, y, z, core):
    return (x * 4 + (z // 4) * 2 + core, lax.rem(z, 4) * 4 + y)


def slot_row(x, y, z):
    z_lo = lax.rem(z, 4)
    return (
        lax.rem(x, 2) * 64
        + lax.rem(y, 2) * 32
        + lax.rem(z_lo, 2) * 16
        + (z // 4) * 8
        + (x // 2) * 4
        + (y // 2) * 2
        + z_lo // 2
    )


def group_of(z):
    z_lo = lax.rem(z, 4)
    return lax.rem(z_lo, 2) * 2 + z_lo // 2


def source_row(x, y, z):
    inner = lax.rem(x, 2) * 16 + lax.rem(y, 2) * 8 + (z // 4) * 4 + (x // 2) * 2 + y // 2
    return group_of(z) * 32 + inner


def exchange_kernel(w_ref, r_ref, raw, packed, pair_send, pair_recv, own_sem, ready, send, recv):
    x, y, z, core = chip()
    bar = pltpu.get_barrier_semaphore()

    def signal(sem, x1, y1, z1, core1):
        pl.semaphore_signal(
            sem, inc=1, device_id=device_of(x1, y1, z1, core1), device_id_type=MESH
        )

    signal(bar, x, y, z, 1 - core)
    for dz in range(1, 8):
        signal(bar, x, y, lax.rem(z + dz, 8), core)
    for d in range(1, 16):
        signal(bar, lax.rem(x + d // 4, 4), lax.rem(y + d % 4, 4), z, core)
    mine = pltpu.make_async_copy(
        w_ref.at[:, pl.ds(core * 128, 128), :], raw.at[core], own_sem
    )
    mine.start()
    pl.semaphore_wait(bar, 23)
    for d in range(1, 16):
        signal(ready, lax.rem(x + d // 4, 4), lax.rem(y + d % 4, 4), z, core)
    swap = pltpu.make_async_remote_copy(
        src_ref=w_ref.at[:, pl.ds((1 - core) * 128, 128), :],
        dst_ref=raw.at[core],
        send_sem=pair_send,
        recv_sem=pair_recv,
        device_id=device_of(x, y, z, 1 - core),
        device_id_type=MESH,
    )
    swap.start()
    mine.wait()
    swap.wait()
    for c in range(2):
        for part in range(2):
            for half in range(2):
                packed[pl.ds(c * 4 + part * 2 + half, 128, stride=8), :] = raw[
                    c, part, :, half * LANES : (half + 1) * LANES
                ]
    pl.semaphore_wait(ready, 15)
    group = group_of(z)
    to_row = source_row(x, y, z) * 8

    def send_one(m, carry):
        dz, dx, dy = (m // 32) + 4 * lax.rem(m // 16, 2), lax.rem(m // 4, 4), lax.rem(m, 4)
        x1, y1, z1 = lax.rem(x + dx, 4), lax.rem(y + dy, 4), lax.rem(z + dz, 8)
        pltpu.make_async_remote_copy(
            src_ref=packed.at[pl.ds(slot_row(x1, y1, z1) * 8, 8), :],
            dst_ref=r_ref.at[pl.ds(to_row, 8), :],
            send_sem=send,
            recv_sem=recv.at[group],
            device_id=device_of(x1, y1, z1, core),
            device_id_type=MESH,
        ).start()
        return carry

    lax.fori_loop(1, 128, send_one, 0)
    pltpu.make_async_copy(
        packed.at[pl.ds(slot_row(x, y, z) * 8, 8), :], r_ref.at[pl.ds(to_row, 8), :], recv.at[group]
    ).start()
    for g in range(4):
        block = r_ref.at[pl.ds(g * 256, 256), :]
        pltpu.make_async_copy(block, block, recv.at[g]).wait()
    sent = packed.at[pl.ds(0, 1016), :]
    pltpu.make_async_copy(sent, sent, send).wait()


def exchange(weights):
    return pl.pallas_call(
        exchange_kernel,
        out_shape=jax.ShapeDtypeStruct((1024, LANES), jnp.float32),
        in_specs=[pl.BlockSpec(memory_space=pl.ANY)],
        out_specs=pl.BlockSpec(memory_space=pltpu.VMEM),
        scratch_shapes=[
            pltpu.VMEM((2, 2, 128, 256), jnp.float32),
            pltpu.VMEM((1024, LANES), jnp.float32),
            pltpu.SemaphoreType.DMA,
            pltpu.SemaphoreType.DMA,
            pltpu.SemaphoreType.DMA,
            pltpu.SemaphoreType.REGULAR,
            pltpu.SemaphoreType.DMA,
            pltpu.SemaphoreType.DMA((4,)),
        ],
        compiler_params=pltpu.CompilerParams(collective_id=0, has_side_effects=True),
    )(weights)


PLACE = {0: 5, 2: 4, 4: 3, 1: 2, 3: 1, 5: 0}
PLACE6 = {0: 5, 2: 4, 4: 3, 1: 2, 3: 1, 5: 0}
PLACE7 = {0: 6, 2: 5, 4: 4, 6: 3, 1: 2, 3: 1, 5: 0}


def bit_of(index, place):
    return jnp.bitwise_and(lax.shift_right_logical(index, place), 1)


def full_index(n, row):
    place = PLACE[n]
    if place >= 3:
        high = lax.shift_right_logical(row, place)
        return lax.shift_left(high, place + 1) + jnp.bitwise_and(row, 2**place - 1)
    per = 5 - place
    return lax.shift_left(jnp.bitwise_and(row, 2**per - 1), place + 1) + lax.shift_right_logical(row, per)


def center(own, js):
    total = own.astype(jnp.float32) * 16.0 - 128.0
    width = 16.0
    for j in js:
        width = width / 2.0
        total = total + (j.astype(jnp.float32) if hasattr(j, "astype") else float(j)) * width
    return total + width / 2.0


def target_center(n, jbits, own):
    first = center(own[0], [jbits[m] for m in range(0, n + 1, 2)])
    second = center(own[1], [jbits[m] for m in range(1, n + 1, 2)])
    return first, second, jnp.sqrt(first * first + second * second)


def shifts(point, axis, slow):
    cos, sin = unit(point)
    if axis == 0:
        return slow[0] + slow[1] * sin
    return slow[2] * cos


def level_table(n, rows, jbits, bbits, own, z, slow, store):
    axis = n % 2
    done = n // 2
    width = 2.0**done / 16.0
    corner = 0.0
    for m in range(n + 2, 8, 2):
        corner = corner + bbits[m].astype(jnp.float32) * (2.0 ** (m // 2) / 16.0)
    last = target_center(n - 2, jbits, own) if n >= 2 else None
    for j in range(2):
        jnew = dict(jbits)
        jnew[n] = j
        new = target_center(n, jnew, own)
        if last is None:
            step_k, step_r = -new[axis], -new[2]
        else:
            step_k, step_r = last[axis] - new[axis], last[2] - new[2]
        for half in range(2 if axis == 0 else 1):
            for c in range(2):
                point = corner + width * (c + z[half])
                turns = point * step_k + shifts(point, axis, slow) * step_r
                store(c, j, half, unit(turns))


def merge(n, children, phases, matrix, rows):
    stacked = []
    for j in range(2):
        cols = ([], [])
        for c in range(2):
            for half in range(2):
                cos, sin = phases(c, j, half if n % 2 == 0 else 0)
                re, im = children[c][0][half], children[c][1][half]
                cols[0].append(re * cos - im * sin)
                cols[1].append(re * sin + im * cos)
        stacked += [jnp.concatenate(cols[0], axis=1), jnp.concatenate(cols[1], axis=1)]
    full = jnp.concatenate(stacked, axis=0)
    high = full.astype(jnp.bfloat16)
    low = (full - high.astype(jnp.float32)).astype(jnp.bfloat16)
    out = jnp.dot(
        jnp.concatenate([high, high, low], axis=1), matrix, preferred_element_type=jnp.float32
    )
    return lambda j, part, half: out[
        (2 * j + part) * rows : (2 * j + part + 1) * rows, half * LANES : (half + 1) * LANES
    ]


def levels_kernel(r_ref, slow_ref, even_ref, odd_ref, o_ref, state, mid, tab, tab6, tab7, last):
    d = own_bits()
    own = (
        d[0] * 8 + d[2] * 4 + d[4] * 2 + d[6],
        d[1] * 8 + d[3] * 4 + d[5] * 2 + d[7],
    )
    slow = [slow_ref[0], slow_ref[1], slow_ref[2]]
    mats = (even_ref, odd_ref)

    def nodes(axis, rows):
        out = []
        for half in range(2 if axis == 0 else 1):
            lane = lax.broadcasted_iota(jnp.int32, (rows, LANES), 1)
            t = lax.shift_right_logical(lane, 4) + 8 * half if axis == 0 else jnp.bitwise_and(lane, 15)
            out.append(0.5 - 0.5 * unit((2.0 * t.astype(jnp.float32) + 1.0) / 64.0)[0])
        return out

    z32 = (nodes(0, 32), nodes(1, 32))
    row = lax.broadcasted_iota(jnp.int32, (32, LANES), 0)
    for n in range(6):
        index = full_index(n, row)
        jbits = {m: bit_of(index, PLACE[m]) for m in range(n)}

        def one_key(key, carry, n=n, index=index, jbits=jbits):
            bbits = {m: bit_of(index, PLACE[m]) for m in range(n + 1, 6)}
            bbits[6] = bbits[7] = key

            def store(c, j, half, value):
                tab[n, key, c, j, half, 0] = value[0]
                tab[n, key, c, j, half, 1] = value[1]

            level_table(n, 32, jbits, bbits, own, z32[n % 2], slow, store)
            return carry

        lax.fori_loop(0, 2, one_key, 0)

    row = lax.broadcasted_iota(jnp.int32, (64, LANES), 0)

    def store6(c, j, half, value):
        tab6[c, j, half, 0] = value[0]
        tab6[c, j, half, 1] = value[1]

    level_table(
        6, 64, {m: bit_of(row, PLACE6[m]) for m in range(6)}, {}, own, nodes(0, 64), slow, store6
    )
    row = lax.broadcasted_iota(jnp.int32, (128, LANES), 0)

    def store7(c, j, half, value):
        tab7[c, j, 0] = value[0]
        tab7[c, j, 1] = value[1]

    jbits7 = {m: bit_of(row, PLACE7[m]) for m in range(7)}
    level_table(7, 128, jbits7, {}, own, nodes(1, 128), slow, store7)

    def group(g, carry):
        keys = (g // 2, lax.rem(g, 2))
        for n in range(6):
            place = PLACE[n]
            if place >= 3:
                size, stride = 2**place, 1
                starts = [k * 2 * size for k in range(32 // size)]
            else:
                size, stride = 32 >> place, 2 ** (place + 1)
                starts = list(range(2**place))

            def pick(c, part, half, starts=starts, size=size, stride=stride, place=place, n=n):
                if n == 0:
                    return r_ref[pl.ds(g * 256 + c * 4 + part * 2 + half, 32, stride=8), :]
                return jnp.concatenate(
                    [
                        state[g, part, half, pl.ds(s + c * 2**place, size, stride=stride), :]
                        for s in starts
                    ]
                )

            children = [
                [[pick(c, part, half) for half in range(2)] for part in range(2)] for c in range(2)
            ]
            key = keys[n % 2]
            out = merge(
                n,
                children,
                lambda c, j, half, n=n, key=key: (
                    tab[n, key, c, j, half, 0],
                    tab[n, key, c, j, half, 1],
                ),
                mats[n % 2][...],
                32,
            )
            for j in range(2):
                for part in range(2):
                    for half in range(2):
                        block = out(j, part, half)
                        for k, s in enumerate(starts):
                            state[g, part, half, pl.ds(s + j * 2**place, size, stride=stride), :] = (
                                block[k * size : (k + 1) * size]
                            )
        return carry

    lax.fori_loop(0, 4, group, 0)

    for b7 in range(2):
        children = [
            [[state[2 * c + b7, part, half] for half in range(2)] for part in range(2)]
            for c in range(2)
        ]
        out = merge(
            6,
            children,
            lambda c, j, half: (tab6[c, j, half, 0], tab6[c, j, half, 1]),
            even_ref[...],
            64,
        )
        for j in range(2):
            for part in range(2):
                for half in range(2):
                    block = out(j, part, half)
                    for k in range(8):
                        mid[b7, part, half, pl.ds(k * 16 + j * 8, 8), :] = block[k * 8 : k * 8 + 8]

    children = [
        [[mid[c, part, half] for half in range(2)] for part in range(2)] for c in range(2)
    ]
    out = merge(
        7, children, lambda c, j, half: (tab7[c, j, 0], tab7[c, j, 1]), odd_ref[...], 128
    )
    first = target_center(6, jbits7, own)
    z_first, z_second = nodes(0, 128), nodes(1, 128)[0]
    for j in range(2):
        second = target_center(7, {**jbits7, 7: j}, own)
        tail = z_second * second[1] + shifts(z_second, 1, slow) * second[2]
        for half in range(2):
            point = z_first[half]
            turns = point * first[0] + shifts(point, 0, slow) * first[2] + tail
            cos, sin = unit(turns)
            re, im = out(j, 0, half), out(j, 1, half)
            last[0, half, pl.ds(j, 128, stride=2), :] = re * cos - im * sin
            last[1, half, pl.ds(j, 128, stride=2), :] = re * sin + im * cos
    for part in range(2):
        for half in range(2):
            o_ref[part, :, half * LANES : (half + 1) * LANES] = last[part, half]


def levels(received, slowness_terms):
    vmem = pl.BlockSpec(memory_space=pltpu.VMEM)
    return pl.pallas_call(
        levels_kernel,
        out_shape=jax.ShapeDtypeStruct((2, 256, 256), jnp.float32),
        in_specs=[vmem, pl.BlockSpec(memory_space=pltpu.SMEM), vmem, vmem],
        out_specs=vmem,
        scratch_shapes=[
            pltpu.VMEM((4, 2, 2, 64, LANES), jnp.float32),
            pltpu.VMEM((2, 2, 2, 128, LANES), jnp.float32),
            pltpu.VMEM((6, 2, 2, 2, 2, 2, 32, LANES), jnp.float32),
            pltpu.VMEM((2, 2, 2, 2, 64, LANES), jnp.float32),
            pltpu.VMEM((2, 2, 2, 128, LANES), jnp.float32),
            pltpu.VMEM((2, 2, 256, LANES), jnp.float32),
        ],
        compiler_params=pltpu.CompilerParams(vmem_limit_bytes=32 * 2**20),
    )(received, slowness_terms, jnp.asarray(split_matrix(0)), jnp.asarray(split_matrix(1)))


def local(weights, slowness_terms):
    received = exchange(weights.reshape(2, 256, 256))
    return levels(received, slowness_terms).reshape(weights.shape)


def solution(mesh):
    return jax.shard_map(
        local,
        mesh=mesh,
        in_specs=(P(None, "src", "tgt", None, None), P()),
        out_specs=P(None, "src", "tgt", None, None),
        check_vma=False,
    )
```

profile of v0, /device:TPU:1, one launch (start us, length us, event | category | flops | bytes accessed | tf_op | source)
XLA Modules:
  0.0 46.0 jit_solution(17723040670733399393)
XLA Ops:
  0.0 0.0 copy-start.1
  0.0 0.0 copy-start.3
  0.0 30.0 %shard_map.46.r_ref = f32[1024,128]{1,0:T(8,128)} custom-call(f32[2,256,256]{2,1,0:T(8,128)} %bitcast.4), custom_call_target="tpu_custom_call" | custom-call | tf_op jit(solution)/shard_map/pallas_call | solution.py:180
  30.0 0.0 copy-done.1
  30.0 0.0 copy-done.3
  30.0 0.0 copy-start
  30.0 1.0 %copy-done = f32[1024,128]{1,0:T(8,128)S(1)} copy-done((f32[1024,128]{1,0:T(8,128)S(1)}, f32[1024,128]{1,0:T(8,128)}, u32[]{:S(2)}) %copy-start) | copy-done | bytes 524312
  31.1 0.0 copy-start.2
  31.1 1.1 %copy-done.2 = bf16[1536,256]{1,0:T(8,128)(2,1)S(1)} copy-done((bf16[1536,256]{1,0:T(8,128)(2,1)S(1)}, bf16[1536,256]{1,0:T(8,128)(2,1)}, u32[]{:S(2)}) %copy-start.2) | copy-done | bytes 786456
  32.2 13.8 %shard_map.47 = f32[2,256,256]{2,1,0:T(8,128)} custom-call(f32[1024,128]{1,0:T(8,128)S(1)} %copy-done, f32[3]{0:T(128)S(1)} %copy-done.3, bf16[1536,256]{1,0:T(8,128)(2,1)S(1)} %copy-done.2, bf16[1536,256]{1,0:T(8,128)(2,1)S(1)} %copy-done.1), custom_call_target="tpu_custom_call" | custom-call | tf_op jit(solution)/shard_map/pallas_call | solution.py:429
Async XLA Ops:
  0.0 30.0 %copy-start.1 = (bf16[1536,256]{1,0:T(8,128)(2,1)S(1)}, bf16[1536,256]{1,0:T(8,128)(2,1)}, u32[]{:S(2)}) copy-start(bf16[1536,256]{1,0:T(8,128)(2,1)} %constant.5.clone.odd_ref) | copy-start | bytes 2359300
  0.0 30.0 %copy-start.3 = (f32[3]{0:T(128)S(1)}, f32[3]{0:T(128)}, u32[]{:S(2)}) copy-start(f32[3]{0:T(128)} %slow_ref.1) | copy-start | bytes 40
  30.0 1.0 %copy-start = (f32[1024,128]{1,0:T(8,128)S(1)}, f32[1024,128]{1,0:T(8,128)}, u32[]{:S(2)}) copy-start(f32[1024,128]{1,0:T(8,128)} %shard_map.46.r_ref) | copy-start | bytes 1572868
  31.1 1.1 %copy-start.2 = (bf16[1536,256]{1,0:T(8,128)(2,1)S(1)}, bf16[1536,256]{1,0:T(8,128)(2,1)}, u32[]{:S(2)}) copy-start(bf16[1536,256]{1,0:T(8,128)(2,1)} %constant.4.clone.even_ref) | copy-start | bytes 2359300
where the time goes:
time: 46.1 us; the launch traced here: 46 us
  Pallas kernels  43.7 us (95%)
  local copies, waits for them, and re-layouts  2.17 us (5%)
    pallas_call x1, Pallas kernels, exchange(): pl.pallas_call(exchange_kernel, out_shape=jax.ShapeDtypeStruct((1024, LAN...  30 us
    pallas_call x1, Pallas kernels, levels(): pl.pallas_call(levels_kernel, out_shape=jax.ShapeDtypeStruct((2, 256, 256...  13.8 us
    unnamed x8, local copies, waits for them, and re-layouts  2.17 us

commit v1 on v0

v1 whole, which is shorter than its diff:
```python
import math

import jax
import jax.numpy as jnp
import numpy as np
from jax import lax
from jax.experimental import pallas as pl
from jax.experimental.pallas import tpu as pltpu
from jax.sharding import PartitionSpec as P

MESH = pl.DeviceIdType.MESH
NODES = 16
LANES = 128
PERIOD = 2.0 * math.pi


def nodes_np():
    t = np.arange(NODES, dtype=np.float64)
    return 0.5 - 0.5 * np.cos((2.0 * t + 1.0) * math.pi / (2 * NODES))


def merge_matrix(axis):
    z = nodes_np()
    eye = np.eye(NODES)
    blocks = []
    for c in range(2):
        at = (c + z) / 2.0
        lag = np.ones((NODES, NODES))
        for t in range(NODES):
            for m in range(NODES):
                if m != t:
                    lag[:, t] *= (at - z[m]) / (z[t] - z[m])
        if axis == 0:
            full = lag[:, None, :, None] * eye[None, :, None, :]
        else:
            full = eye[:, None, :, None] * lag[None, :, None, :]
        blocks.append(full.reshape(256, 256))
    return np.concatenate(blocks)


def even_matrix():
    return merge_matrix(0).astype(np.float32)


def odd_matrix():
    full = merge_matrix(1)
    block = np.concatenate([full[:LANES, :LANES], full[256 : 256 + LANES, :LANES]])
    return block.astype(np.float32)


def fit(fn, count):
    u = 0.125 - 0.125 * np.cos((np.arange(400) + 0.5) * math.pi / 400)
    c = np.polynomial.chebyshev.Chebyshev.fit(u, fn(np.sqrt(u)), count - 1, domain=[0, 0.25])
    return [float(v) for v in c.convert(kind=np.polynomial.Polynomial, domain=[-1, 1]).coef]


SIN_FIT = fit(lambda f: np.sin(math.pi * f) / f, 5)
COS_FIT = fit(lambda f: np.cos(math.pi * f), 6)


def horner(u, coef):
    acc = jnp.full_like(u, coef[-1])
    for v in coef[-2::-1]:
        acc = acc * u + v
    return acc


def unit(turns):
    f = turns - jnp.round(turns)
    u = f * f
    s = f * horner(u, SIN_FIT)
    c = horner(u, COS_FIT)
    return 1.0 - 2.0 * s * s, 2.0 * s * c


def own_bits():
    src, tgt = lax.axis_index("src"), lax.axis_index("tgt")
    bits = [lax.rem(src // 2**m, 2) for m in range(4)]
    return bits + [lax.rem(tgt // 2**m, 2) for m in range(4)]


def chip():
    src, tgt = lax.axis_index("src"), lax.axis_index("tgt")
    x, z_hi, core = src // 4, lax.rem(src // 2, 2), lax.rem(src, 2)
    return x, lax.rem(tgt, 4), z_hi * 4 + tgt // 4, core


def device_of(x, y, z, core):
    return (x * 4 + (z // 4) * 2 + core, lax.rem(z, 4) * 4 + y)


def slot_row(x, y, z):
    z_lo = lax.rem(z, 4)
    return (
        lax.rem(x, 2) * 64
        + lax.rem(y, 2) * 32
        + lax.rem(z_lo, 2) * 16
        + (z // 4) * 8
        + (x // 2) * 4
        + (y // 2) * 2
        + z_lo // 2
    )


def group_of(z):
    z_lo = lax.rem(z, 4)
    return lax.rem(z_lo, 2) * 2 + z_lo // 2


def source_row(x, y, z):
    inner = lax.rem(x, 2) * 16 + lax.rem(y, 2) * 8 + (z // 4) * 4 + (x // 2) * 2 + y // 2
    return group_of(z) * 32 + inner


PLACE = {0: 5, 2: 4, 4: 3, 1: 2, 3: 1, 5: 0}
PLACE7 = {0: 6, 2: 5, 4: 4, 6: 3, 1: 2, 3: 1, 5: 0}


def bit_of(index, place):
    return jnp.bitwise_and(lax.shift_right_logical(index, place), 1)


def full_index(n, row):
    place = PLACE[n]
    if place >= 3:
        high = lax.shift_right_logical(row, place)
        return lax.shift_left(high, place + 1) + jnp.bitwise_and(row, 2**place - 1)
    per = 5 - place
    return lax.shift_left(jnp.bitwise_and(row, 2**per - 1), place + 1) + lax.shift_right_logical(row, per)


def center(own, js):
    total = own.astype(jnp.float32) * 16.0 - 128.0
    width = 16.0
    for j in js:
        width = width / 2.0
        total = total + (j.astype(jnp.float32) if hasattr(j, "astype") else float(j)) * width
    return total + width / 2.0


def target_center(n, jbits, own):
    first = center(own[0], [jbits[m] for m in range(0, n + 1, 2)])
    second = center(own[1], [jbits[m] for m in range(1, n + 1, 2)])
    return first, second, jnp.sqrt(first * first + second * second)


def shifts(point, axis, slow):
    cos, sin = unit(point)
    if axis == 0:
        return slow[0] + slow[1] * sin
    return slow[2] * cos


def level_table(n, rows, jbits, bbits, own, z, slow, store):
    axis = n % 2
    done = n // 2
    width = 2.0**done / 16.0
    corner = 0.0
    for m in range(n + 2, 8, 2):
        corner = corner + bbits[m].astype(jnp.float32) * (2.0 ** (m // 2) / 16.0)
    last = target_center(n - 2, jbits, own) if n >= 2 else None
    for j in range(2):
        jnew = dict(jbits)
        jnew[n] = j
        new = target_center(n, jnew, own)
        if last is None:
            step_k, step_r = -new[axis], -new[2]
        else:
            step_k, step_r = last[axis] - new[axis], last[2] - new[2]
        for half in range(2 if axis == 0 else 1):
            for c in range(2):
                point = corner + width * (c + z[half])
                turns = point * step_k + shifts(point, axis, slow) * step_r
                store(c, j, half, unit(turns))


def halves_first(n, children, phases):
    out = []
    for j in range(2):
        real, imag = [], []
        for c in range(2):
            pairs = [phases(c, j, half if n % 2 == 0 else 0) for half in range(2)]
            re, im = children[c]
            real.append([re[h] * pairs[h][0] - im[h] * pairs[h][1] for h in range(2)])
            imag.append([re[h] * pairs[h][1] + im[h] * pairs[h][0] for h in range(2)])
        out.append((real, imag))
    return out


def high_low(full):
    high = full.astype(jnp.bfloat16)
    return high, (full - high.astype(jnp.float32)).astype(jnp.bfloat16)


def merge(n, blocks, even_ref, odd_ref):
    turned = [halves_first(n, *block) for block in blocks]
    rows = blocks[0][0][0][0][0].shape[0]
    f32 = jnp.float32
    if n % 2 == 0:
        full = jnp.concatenate(
            [
                jnp.concatenate([t[j][part][c][h] for c in range(2) for h in range(2)], axis=1)
                for t in turned
                for j in range(2)
                for part in range(2)
            ]
        )
        count = full.shape[0]
        high, low = high_low(full)
        both = jnp.dot(
            jnp.concatenate([high, low]), even_ref[0:512, :], preferred_element_type=f32
        )
        rest = jnp.dot(high, even_ref[512:1024, :], preferred_element_type=f32)
        total = both[:count] + (both[count:] + rest)

        def out(block, j, part, half):
            first = (block * 4 + 2 * j + part) * rows
            return total[first : first + rows, half * LANES : (half + 1) * LANES]

        return out
    full = jnp.concatenate(
        [
            jnp.concatenate([t[j][part][c][h] for c in range(2)], axis=1)
            for t in turned
            for j in range(2)
            for part in range(2)
            for h in range(2)
        ]
    )
    count = full.shape[0]
    high, low = high_low(full)
    both = jnp.dot(jnp.concatenate([high, low]), odd_ref[...], preferred_element_type=f32)
    total = both[:count, :LANES] + (both[:count, LANES:] + both[count:, :LANES])

    def out(block, j, part, half):
        first = (block * 8 + 4 * j + 2 * part + half) * rows
        return total[first : first + rows]

    return out


def lane_nodes(axis, rows):
    out = []
    for half in range(2 if axis == 0 else 1):
        lane = lax.broadcasted_iota(jnp.int32, (rows, LANES), 1)
        t = lax.shift_right_logical(lane, 4) + 8 * half if axis == 0 else jnp.bitwise_and(lane, 15)
        out.append(0.5 - 0.5 * unit((2.0 * t.astype(jnp.float32) + 1.0) / 64.0)[0])
    return out


def fill_tables(own, slow, tab, tab6, tab7):
    nodes = (lane_nodes(0, 32), lane_nodes(1, 32))
    row = lax.broadcasted_iota(jnp.int32, (32, LANES), 0)
    for n in range(6):
        index = full_index(n, row)
        jbits = {m: bit_of(index, PLACE[m]) for m in range(n)}

        def one_key(key, carry, n=n, index=index, jbits=jbits):
            bbits = {m: bit_of(index, PLACE[m]) for m in range(n + 1, 6)}
            bbits[6] = bbits[7] = key

            def store(c, j, half, value):
                tab[n, key, c, j, half, 0] = value[0]
                tab[n, key, c, j, half, 1] = value[1]

            level_table(n, 32, jbits, bbits, own, nodes[n % 2], slow, store)
            return carry

        lax.fori_loop(0, 2, one_key, 0)
    row = lax.broadcasted_iota(jnp.int32, (64, LANES), 0)
    jbits = {m: bit_of(row, PLACE[m]) for m in range(6)}

    def store6(c, j, half, value):
        tab6[c, j, half, 0] = value[0]
        tab6[c, j, half, 1] = value[1]

    level_table(6, 64, jbits, {}, own, lane_nodes(0, 64), slow, store6)
    row = lax.broadcasted_iota(jnp.int32, (128, LANES), 0)
    jbits = {m: bit_of(row, PLACE7[m]) for m in range(7)}

    def store7(c, j, half, value):
        tab7[c, j, 0] = value[0]
        tab7[c, j, 1] = value[1]

    level_table(7, 128, jbits, {}, own, lane_nodes(1, 128), slow, store7)


def fill_last(own, slow, last):
    row = lax.broadcasted_iota(jnp.int32, (128, LANES), 0)
    jbits = {m: bit_of(row, PLACE7[m]) for m in range(7)}
    first = target_center(6, jbits, own)
    z_first, z_second = lane_nodes(0, 128), lane_nodes(1, 128)[0]
    for j in range(2):
        second = target_center(7, {**jbits, 7: j}, own)
        tail = z_second * second[1] + shifts(z_second, 1, slow) * second[2]
        for half in range(2):
            point = z_first[half]
            cos, sin = unit(point * first[0] + shifts(point, 0, slow) * first[2] + tail)
            last[j, half, 0] = cos
            last[j, half, 1] = sin


def early_levels(groups, r_ref, state, tab, even_ref, odd_ref):
    for n in range(6):
        place = PLACE[n]
        if place >= 3:
            size, stride = 2**place, 1
            starts = [k * 2 * size for k in range(32 // size)]
        else:
            size, stride = 32 >> place, 2 ** (place + 1)
            starts = list(range(2**place))

        def pick(g, c, part, half, n=n, place=place, size=size, stride=stride, starts=starts):
            if n == 0:
                return r_ref[pl.ds(g * 256 + c * 4 + part * 2 + half, 32, stride=8), :]
            return jnp.concatenate(
                [
                    state[g, part, half, pl.ds(s + c * 2**place, size, stride=stride), :]
                    for s in starts
                ]
            )

        blocks = []
        for g, b6, b7 in groups:
            children = [
                [[pick(g, c, part, half) for half in range(2)] for part in range(2)]
                for c in range(2)
            ]
            key = b7 if n % 2 else b6

            def phases(c, j, half, n=n, key=key):
                return tab[n, key, c, j, half, 0], tab[n, key, c, j, half, 1]

            blocks.append((children, phases))
        out = merge(n, blocks, even_ref, odd_ref)
        for at, (g, _, _) in enumerate(groups):
            for j in range(2):
                for part in range(2):
                    for half in range(2):
                        block = out(at, j, part, half)
                        for k, s in enumerate(starts):
                            state[
                                g, part, half, pl.ds(s + j * 2**place, size, stride=stride), :
                            ] = block[k * size : (k + 1) * size]


def late_levels(state, mid, tab6, tab7, last, fin, even_ref, odd_ref, o_ref):
    blocks = []
    for b7 in range(2):
        children = [
            [[state[2 * c + b7, part, half] for half in range(2)] for part in range(2)]
            for c in range(2)
        ]
        blocks.append((children, lambda c, j, half: (tab6[c, j, half, 0], tab6[c, j, half, 1])))
    out = merge(6, blocks, even_ref, odd_ref)
    for b7 in range(2):
        for j in range(2):
            for part in range(2):
                for half in range(2):
                    block = out(b7, j, part, half)
                    for k in range(8):
                        mid[b7, part, half, pl.ds(k * 16 + j * 8, 8), :] = block[k * 8 : k * 8 + 8]
    children = [
        [[mid[c, part, half] for half in range(2)] for part in range(2)] for c in range(2)
    ]
    block = (children, lambda c, j, half: (tab7[c, j, 0], tab7[c, j, 1]))
    out = merge(7, [block], even_ref, odd_ref)
    for j in range(2):
        for half in range(2):
            cos, sin = last[j, half, 0], last[j, half, 1]
            re, im = out(0, j, 0, half), out(0, j, 1, half)
            fin[0, half, pl.ds(j, 128, stride=2), :] = re * cos - im * sin
            fin[1, half, pl.ds(j, 128, stride=2), :] = re * sin + im * cos
    for part in range(2):
        for half in range(2):
            o_ref[part, :, half * LANES : (half + 1) * LANES] = fin[part, half]


def kernel(
    w_ref, slow_hbm, even_hbm, odd_hbm, o_ref,
    raw, packed, r_ref, even_raw, odd_raw, even_ref, odd_ref, slow_ref, state, mid, tab, tab6, tab7, last, fin,
    pair_send, pair_recv, own_sem, load_sem, ready, send, recv,
):
    x, y, z, core = chip()
    bar = pltpu.get_barrier_semaphore()

    def signal(sem, x1, y1, z1, core1):
        pl.semaphore_signal(
            sem, inc=1, device_id=device_of(x1, y1, z1, core1), device_id_type=MESH
        )

    signal(bar, x, y, z, 1 - core)
    for dz in range(1, 8):
        signal(bar, x, y, lax.rem(z + dz, 8), core)
    for d in range(1, 16):
        signal(bar, lax.rem(x + d // 4, 4), lax.rem(y + d % 4, 4), z, core)
    mine = pltpu.make_async_copy(
        w_ref.at[:, pl.ds(core * 128, 128), :], raw.at[core], own_sem
    )
    mine.start()
    loads = [
        pltpu.make_async_copy(a, b, load_sem.at[k])
        for k, (a, b) in enumerate(
            [(slow_hbm, slow_ref), (even_hbm, even_raw), (odd_hbm, odd_raw)]
        )
    ]
    for load in loads:
        load.start()
    pl.semaphore_wait(bar, 23)
    for d in range(1, 16):
        signal(ready, lax.rem(x + d // 4, 4), lax.rem(y + d % 4, 4), z, core)
    swap = pltpu.make_async_remote_copy(
        src_ref=w_ref.at[:, pl.ds((1 - core) * 128, 128), :],
        dst_ref=raw.at[core],
        send_sem=pair_send,
        recv_sem=pair_recv,
        device_id=device_of(x, y, z, 1 - core),
        device_id_type=MESH,
    )
    swap.start()
    mine.wait()
    swap.wait()
    for c in range(2):
        for part in range(2):
            for half in range(2):
                packed[pl.ds(c * 4 + part * 2 + half, 128, stride=8), :] = raw[
                    c, part, :, half * LANES : (half + 1) * LANES
                ]
    pl.semaphore_wait(ready, 15)
    group = group_of(z)
    to_row = source_row(x, y, z) * 8

    def send_to(dx, dy, dz):
        x1, y1, z1 = lax.rem(x + dx, 4), lax.rem(y + dy, 4), lax.rem(z + dz, 8)
        pltpu.make_async_remote_copy(
            src_ref=packed.at[pl.ds(slot_row(x1, y1, z1) * 8, 8), :],
            dst_ref=r_ref.at[pl.ds(to_row, 8), :],
            send_sem=send,
            recv_sem=recv.at[group],
            device_id=device_of(x1, y1, z1, core),
            device_id_type=MESH,
        ).start()

    def send_a(m, carry):
        send_to(m // 8, lax.rem(m // 2, 4), 4 * lax.rem(m, 2))
        return carry

    def send_b(m, carry):
        send_to(m // 8, lax.rem(m // 2, 4), 2 + 4 * lax.rem(m, 2))
        return carry

    def send_c(m, carry):
        send_to(m // 16, lax.rem(m // 4, 4), 1 + 2 * lax.rem(m, 4))
        return carry

    pltpu.make_async_copy(
        packed.at[pl.ds(slot_row(x, y, z) * 8, 8), :], r_ref.at[pl.ds(to_row, 8), :], recv.at[group]
    ).start()
    lax.fori_loop(1, 32, send_a, 0)
    lax.fori_loop(0, 32, send_b, 0)
    lax.fori_loop(0, 64, send_c, 0)

    for load in loads:
        load.wait()
    even_ref[0:512, :], even_ref[512:1024, :] = high_low(even_raw[...])
    odd_ref[:, 0:LANES], odd_ref[:, LANES : 2 * LANES] = high_low(odd_raw[...])
    d = own_bits()
    own = (
        d[0] * 8 + d[2] * 4 + d[4] * 2 + d[6],
        d[1] * 8 + d[3] * 4 + d[5] * 2 + d[7],
    )
    slow = [slow_ref[0], slow_ref[1], slow_ref[2]]
    fill_tables(own, slow, tab, tab6, tab7)
    fill_last(own, slow, last)

    def arrive(g):
        block = r_ref.at[pl.ds(g * 256, 256), :]
        pltpu.make_async_copy(block, block, recv.at[g]).wait()

    b6, b7 = d[6], d[7]

    def near(k, carry):
        far7 = k + b7 - 2 * k * b7
        g = 2 * b6 + far7
        arrive(g)
        early_levels([(g, b6, far7)], r_ref, state, tab, even_ref, odd_ref)
        return carry

    lax.fori_loop(0, 2, near, 0)
    g = 2 * (1 - b6)
    arrive(g)
    arrive(g + 1)
    early_levels([(g, 1 - b6, 0), (g + 1, 1 - b6, 1)], r_ref, state, tab, even_ref, odd_ref)
    late_levels(state, mid, tab6, tab7, last, fin, even_ref, odd_ref, o_ref)
    sent = packed.at[pl.ds(0, 1016), :]
    pltpu.make_async_copy(sent, sent, send).wait()


def butterfly(weights, slowness_terms):
    hbm = pl.BlockSpec(memory_space=pltpu.HBM)
    f32, bf16 = jnp.float32, jnp.bfloat16
    return pl.pallas_call(
        kernel,
        out_shape=pltpu.VMEM((2, 256, 256), f32),
        in_specs=[hbm] * 4,
        out_specs=pl.BlockSpec(memory_space=pltpu.VMEM),
        scratch_shapes=[
            pltpu.VMEM((2, 2, 128, 256), f32),
            pltpu.VMEM((1024, LANES), f32),
            pltpu.VMEM((1024, LANES), f32),
            pltpu.VMEM((512, 256), f32),
            pltpu.VMEM((256, LANES), f32),
            pltpu.VMEM((1024, 256), bf16),
            pltpu.VMEM((256, 256), bf16),
            pltpu.SMEM((3,), f32),
            pltpu.VMEM((4, 2, 2, 64, LANES), f32),
            pltpu.VMEM((2, 2, 2, 128, LANES), f32),
            pltpu.VMEM((6, 2, 2, 2, 2, 2, 32, LANES), f32),
            pltpu.VMEM((2, 2, 2, 2, 64, LANES), f32),
            pltpu.VMEM((2, 2, 2, 128, LANES), f32),
            pltpu.VMEM((2, 2, 2, 128, LANES), f32),
            pltpu.VMEM((2, 2, 256, LANES), f32),
            pltpu.SemaphoreType.DMA,
            pltpu.SemaphoreType.DMA,
            pltpu.SemaphoreType.DMA,
            pltpu.SemaphoreType.DMA((3,)),
            pltpu.SemaphoreType.REGULAR,
            pltpu.SemaphoreType.DMA,
            pltpu.SemaphoreType.DMA((4,)),
        ],
        compiler_params=pltpu.CompilerParams(
            collective_id=0, has_side_effects=True, vmem_limit_bytes=48 * 2**20
        ),
    )(
        *(
            pltpu.with_memory_space_constraint(a, pltpu.HBM)
            for a in (
                weights,
                slowness_terms,
                jnp.asarray(even_matrix()),
                jnp.asarray(odd_matrix()),
            )
        )
    )


def local(weights, slowness_terms):
    return butterfly(weights.reshape(2, 256, 256), slowness_terms).reshape(weights.shape)


def solution(mesh):
    return jax.shard_map(
        local,
        mesh=mesh,
        in_specs=(P(None, "src", "tgt", None, None), P()),
        out_specs=P(None, "src", "tgt", None, None),
        check_vma=False,
    )
```

time: 46.1 us -> 33.6 us (0.73)
  Pallas kernels: 43.7 us -> 32.7 us
  local copies, waits for them, and re-layouts: 2.17 us -> 0.8 us
    pallas_call x2 -> x1, Pallas kernels: 43.7 us -> 32.7 us  [butterfly(): pl.pallas_call(kernel, out_shape=pltpu.VMEM((2, 256, 256), f32), in_specs...]
    unnamed x8 -> x1, local copies, waits for them, and re-layouts: 2.17 us -> 0.8 us
where the time goes in v1:
time: 33.6 us; the launch traced here: 33.5 us
  Pallas kernels  32.7 us (97%)
  local copies, waits for them, and re-layouts  0.8 us (2%)
    pallas_call x1, Pallas kernels, butterfly(): pl.pallas_call(kernel, out_shape=pltpu.VMEM((2, 256, 256), f32), in_specs...  32.7 us
    unnamed x1, local copies, waits for them, and re-layouts  0.8 us

profile of v1, /device:TPU:1, one launch (start us, length us, event | category | flops | bytes accessed | tf_op | source)
XLA Modules:
  0.0 33.5 jit_solution(10754852409920887990)
XLA Ops:
  0.0 32.7 %shard_map.46 = f32[2,256,256]{2,1,0:T(8,128)S(1)} custom-call(f32[2,256,256]{2,1,0:T(8,128)} %bitcast.5, f32[3]{0:T(128)} %slow_hbm.1, f32[512,256]{1,0:T(8,128)} %constant.4.clone.even_hbm, f32[256,128]{1,0:T(8,128)} %constant.5.clone.odd_hbm), custom_call_target="tpu_custom_call" | custom-call | tf_op jit(solution)/shard_map/pallas_call | solution.py:502
  32.7 0.8 %copy.7 = f32[2,1,1,256,256]{4,3,2,1,0:T(8,128)} copy(f32[2,1,1,256,256]{4,3,2,1,0:T(8,128)S(1)} %bitcast.4) | data formatting | bytes 1048576

commit v2 on v1

v2 whole, which is shorter than its diff:
```python
import math

import jax
import jax.numpy as jnp
import numpy as np
from jax import lax
from jax.experimental import pallas as pl
from jax.experimental.pallas import tpu as pltpu
from jax.sharding import PartitionSpec as P

MESH = pl.DeviceIdType.MESH
NODES = 16
LANES = 128
PERIOD = 2.0 * math.pi


def nodes_np():
    t = np.arange(NODES, dtype=np.float64)
    return 0.5 - 0.5 * np.cos((2.0 * t + 1.0) * math.pi / (2 * NODES))


def merge_matrix(axis):
    z = nodes_np()
    eye = np.eye(NODES)
    blocks = []
    for c in range(2):
        at = (c + z) / 2.0
        lag = np.ones((NODES, NODES))
        for t in range(NODES):
            for m in range(NODES):
                if m != t:
                    lag[:, t] *= (at - z[m]) / (z[t] - z[m])
        if axis == 0:
            full = lag[:, None, :, None] * eye[None, :, None, :]
        else:
            full = eye[:, None, :, None] * lag[None, :, None, :]
        blocks.append(full.reshape(256, 256))
    return np.concatenate(blocks)


def even_matrix():
    return merge_matrix(0).astype(np.float32)


def odd_matrix():
    full = merge_matrix(1)
    block = np.concatenate([full[:LANES, :LANES], full[256 : 256 + LANES, :LANES]])
    return block.astype(np.float32)


def fit(fn, count):
    u = 0.125 - 0.125 * np.cos((np.arange(400) + 0.5) * math.pi / 400)
    c = np.polynomial.chebyshev.Chebyshev.fit(u, fn(np.sqrt(u)), count - 1, domain=[0, 0.25])
    return [float(v) for v in c.convert(kind=np.polynomial.Polynomial, domain=[-1, 1]).coef]


SIN_FIT = fit(lambda f: np.sin(math.pi * f) / f, 5)
COS_FIT = fit(lambda f: np.cos(math.pi * f), 6)


def horner(u, coef):
    acc = jnp.full_like(u, coef[-1])
    for v in coef[-2::-1]:
        acc = acc * u + v
    return acc


def unit(turns):
    f = turns - jnp.round(turns)
    u = f * f
    s = f * horner(u, SIN_FIT)
    c = horner(u, COS_FIT)
    return 1.0 - 2.0 * s * s, 2.0 * s * c


def own_bits():
    src, tgt = lax.axis_index("src"), lax.axis_index("tgt")
    bits = [lax.rem(src // 2**m, 2) for m in range(4)]
    return bits + [lax.rem(tgt // 2**m, 2) for m in range(4)]


def chip():
    src, tgt = lax.axis_index("src"), lax.axis_index("tgt")
    x, z_hi, core = src // 4, lax.rem(src // 2, 2), lax.rem(src, 2)
    return x, lax.rem(tgt, 4), z_hi * 4 + tgt // 4, core


def along_x(x, step):
    a = lax.rem(x + step, 4)
    return a * 4, lax.rem(a, 2) * 64 + (a // 2) * 4


def along_y(y, step):
    a = lax.rem(y + step, 4)
    return a, lax.rem(a, 2) * 32 + (a // 2) * 2


def along_z(z, step, core):
    a = lax.rem(z + step, 8)
    low, high = lax.rem(a, 4), a // 4
    return high * 2 + core, low * 4, lax.rem(low, 2) * 16 + high * 8 + low // 2


def tile_in_group(d):
    return d[2] * 16 + d[6] * 8 + d[1] * 4 + d[3] * 2 + d[7]


PLACE = {0: 5, 2: 4, 6: 3, 1: 2, 3: 1, 7: 0}


def bit_of(index, place):
    return jnp.bitwise_and(lax.shift_right_logical(index, place), 1)


def full_index(n, row):
    place = PLACE[n]
    if place >= 3:
        high = lax.shift_right_logical(row, place)
        return lax.shift_left(high, place + 1) + jnp.bitwise_and(row, 2**place - 1)
    per = 5 - place
    return lax.shift_left(jnp.bitwise_and(row, 2**per - 1), place + 1) + lax.shift_right_logical(row, per)


def center(own, js):
    total = own.astype(jnp.float32) * 16.0 - 128.0
    width = 16.0
    for j in js:
        width = width / 2.0
        total = total + (j.astype(jnp.float32) if hasattr(j, "astype") else float(j)) * width
    return total + width / 2.0


def target_center(n, jbits, own):
    first = center(own[0], [jbits[m] for m in range(0, n + 1, 2)])
    second = center(own[1], [jbits[m] for m in range(1, n + 1, 2)])
    return first, second, jnp.sqrt(first * first + second * second)


def shifts(point, axis, slow):
    cos, sin = unit(point)
    if axis == 0:
        return slow[0] + slow[1] * sin
    return slow[2] * cos


def level_table(n, rows, jbits, bbits, own, z, slow, store):
    axis = n % 2
    done = n // 2
    width = 2.0**done / 16.0
    corner = 0.0
    for m in range(n + 2, 8, 2):
        corner = corner + bbits[m].astype(jnp.float32) * (2.0 ** (m // 2) / 16.0)
    last = target_center(n - 2, jbits, own) if n >= 2 else None
    for j in range(2):
        jnew = dict(jbits)
        jnew[n] = j
        new = target_center(n, jnew, own)
        if last is None:
            step_k, step_r = -new[axis], -new[2]
        else:
            step_k, step_r = last[axis] - new[axis], last[2] - new[2]
        for half in range(2 if axis == 0 else 1):
            for c in range(2):
                point = corner + width * (c + z[half])
                turns = point * step_k + shifts(point, axis, slow) * step_r
                store(c, j, half, unit(turns))


def halves_first(n, children, phases):
    out = []
    for j in range(2):
        real, imag = [], []
        for c in range(2):
            pairs = [phases(c, j, half if n % 2 == 0 else 0) for half in range(2)]
            re, im = children[c]
            real.append([re[h] * pairs[h][0] - im[h] * pairs[h][1] for h in range(2)])
            imag.append([re[h] * pairs[h][1] + im[h] * pairs[h][0] for h in range(2)])
        out.append((real, imag))
    return out


def high_low(full):
    high = full.astype(jnp.bfloat16)
    return high, (full - high.astype(jnp.float32)).astype(jnp.bfloat16)


def merge(n, blocks, even_ref, odd_ref):
    turned = [halves_first(n, *block) for block in blocks]
    rows = blocks[0][0][0][0][0].shape[0]
    f32 = jnp.float32
    if n % 2 == 0:
        full = jnp.concatenate(
            [
                jnp.concatenate([t[j][part][c][h] for c in range(2) for h in range(2)], axis=1)
                for t in turned
                for j in range(2)
                for part in range(2)
            ]
        )
        count = full.shape[0]
        high, low = high_low(full)
        both = jnp.dot(
            jnp.concatenate([high, low]), even_ref[0:512, :], preferred_element_type=f32
        )
        rest = jnp.dot(high, even_ref[512:1024, :], preferred_element_type=f32)
        total = both[:count] + (both[count:] + rest)

        def out(block, j, part, half):
            first = (block * 4 + 2 * j + part) * rows
            return total[first : first + rows, half * LANES : (half + 1) * LANES]

        return out
    full = jnp.concatenate(
        [
            jnp.concatenate([t[j][part][c][h] for c in range(2)], axis=1)
            for t in turned
            for j in range(2)
            for part in range(2)
            for h in range(2)
        ]
    )
    count = full.shape[0]
    high, low = high_low(full)
    both = jnp.dot(jnp.concatenate([high, low]), odd_ref[...], preferred_element_type=f32)
    total = both[:count, :LANES] + (both[:count, LANES:] + both[count:, :LANES])

    def out(block, j, part, half):
        first = (block * 8 + 4 * j + 2 * part + half) * rows
        return total[first : first + rows]

    return out


def lane_nodes(axis, rows):
    out = []
    for half in range(2 if axis == 0 else 1):
        lane = lax.broadcasted_iota(jnp.int32, (rows, LANES), 1)
        t = lax.shift_right_logical(lane, 4) + 8 * half if axis == 0 else jnp.bitwise_and(lane, 15)
        out.append(0.5 - 0.5 * unit((2.0 * t.astype(jnp.float32) + 1.0) / 64.0)[0])
    return out


def keep(table, *lead):
    def store(c, j, half, value):
        table[(*lead, c, j, half, 0)] = value[0]
        table[(*lead, c, j, half, 1)] = value[1]

    return store


def fill_early(own, slow, tab):
    nodes = (lane_nodes(0, 32), lane_nodes(1, 32))
    row = lax.broadcasted_iota(jnp.int32, (32, LANES), 0)
    for n in range(4):
        index = full_index(n, row)
        jbits = {m: bit_of(index, PLACE[m]) for m in range(n)}

        def one_key(key, carry, n=n, index=index, jbits=jbits):
            bbits = {m: bit_of(index, PLACE[m]) for m in (*range(n + 1, 4), 6, 7)}
            bbits[4] = bbits[5] = key
            level_table(n, 32, jbits, bbits, own, nodes[n % 2], slow, keep(tab, n, key))
            return carry

        lax.fori_loop(0, 2, one_key, 0)


def fill_middle(own, slow, tab4, tab5):
    row = lax.broadcasted_iota(jnp.int32, (64, LANES), 0)
    jbits = {m: bit_of(row, PLACE[m]) for m in range(4)}
    level_table(4, 64, jbits, {6: bit_of(row, PLACE[6])}, own, lane_nodes(0, 64), slow, keep(tab4))
    nodes = lane_nodes(1, 64)

    def five(j4, carry):
        bbits = {7: bit_of(row, PLACE[7])}
        level_table(5, 64, {**jbits, 4: j4}, bbits, own, nodes, slow, keep(tab5, j4))
        return carry

    lax.fori_loop(0, 2, five, 0)


def fill_late(own, slow, tab6, tab7, last):
    row32 = lax.broadcasted_iota(jnp.int32, (32, LANES), 0)
    six, seven = full_index(6, row32), full_index(7, row32)
    first_nodes, second_nodes = lane_nodes(0, 32), lane_nodes(1, 32)

    def rest(k, carry):
        j4, j5 = k // 2, lax.rem(k, 2)
        jbits = {m: bit_of(six, PLACE[m]) for m in range(4)}
        jbits.update({4: j4, 5: j5})
        level_table(6, 32, jbits, {}, own, first_nodes, slow, keep(tab6, k))
        jbits = {m: bit_of(seven, PLACE[m]) for m in (0, 1, 2, 3, 6)}
        jbits.update({4: j4, 5: j5})
        level_table(7, 32, jbits, {}, own, second_nodes, slow, keep(tab7, k))
        first = target_center(6, jbits, own)
        z2 = second_nodes[0]
        for j in range(2):
            second = target_center(7, {**jbits, 7: j}, own)
            tail = z2 * second[1] + shifts(z2, 1, slow) * second[2]
            for half in range(2):
                point = first_nodes[half]
                cos, sin = unit(point * first[0] + shifts(point, 0, slow) * first[2] + tail)
                last[k, j, half, 0] = cos
                last[k, j, half, 1] = sin
        return carry

    lax.fori_loop(0, 4, rest, 0)


def row_pattern(place):
    if place >= 3:
        return [k * 2 * 2**place for k in range(32 // 2**place)], 2**place, 1
    return list(range(2**place)), 32 >> place, 2 ** (place + 1)


def read_children(ref, lead, place):
    starts, size, stride = row_pattern(place)
    return [
        [
            [
                jnp.concatenate(
                    [
                        ref[(*lead, part, half, pl.ds(s + c * 2**place, size, stride=stride))]
                        for s in starts
                    ]
                )
                for half in range(2)
            ]
            for part in range(2)
        ]
        for c in range(2)
    ]


def write_siblings(ref, lead, place, out, at):
    starts, size, stride = row_pattern(place)
    for j in range(2):
        for part in range(2):
            for half in range(2):
                block = out(at, j, part, half)
                for k, s in enumerate(starts):
                    ref[(*lead, part, half, pl.ds(s + j * 2**place, size, stride=stride))] = block[
                        k * size : (k + 1) * size
                    ]


def phases_of(table, lead):
    return lambda c, j, half: (table[(*lead, c, j, half, 0)], table[(*lead, c, j, half, 1)])


def early_levels(groups, first, state, tab, even_ref, odd_ref):
    for n in range(4):
        blocks = []
        for b4, b5 in groups:
            g = 2 * b4 + b5
            if n == 0:
                children = [
                    [
                        [
                            first(b4, b5, c, part * 2 + half)
                            for half in range(2)
                        ]
                        for part in range(2)
                    ]
                    for c in range(2)
                ]
            else:
                children = read_children(state, (g,), PLACE[n])
            blocks.append((children, phases_of(tab, (n, b5 if n % 2 else b4))))
        out = merge(n, blocks, even_ref, odd_ref)
        for at, (b4, b5) in enumerate(groups):
            write_siblings(state, (2 * b4 + b5,), PLACE[n], out, at)


QUADS = [(j, part, half) for j in range(2) for part in range(2) for half in range(2)]


def whole(ref, *leads):
    return [
        [[ref[(*lead, part, half)] for half in range(2)] for part in range(2)] for lead in leads
    ]


def level_four(b5, state, mid, tab4, even_ref, odd_ref):
    out = merge(4, [(whole(state, (b5,), (2 + b5,)), phases_of(tab4, ()))], even_ref, odd_ref)
    for j, part, half in QUADS:
        mid[b5, j, part, half] = out(0, j, part, half)


def late_levels(mid, deep, tab5, tab6, tab7, last, fin, even_ref, odd_ref, o_ref):
    blocks = [(whole(mid, (0, j4), (1, j4)), phases_of(tab5, (j4,))) for j4 in range(2)]
    out = merge(5, blocks, even_ref, odd_ref)
    for j4 in range(2):
        for j, part, half in QUADS:
            deep[2 * j4 + j, part, half] = out(j4, j, part, half)
    blocks = [(read_children(deep, (k,), PLACE[6]), phases_of(tab6, (k,))) for k in range(4)]
    out = merge(6, blocks, even_ref, odd_ref)
    for k in range(4):
        write_siblings(deep, (k,), PLACE[6], out, k)
    blocks = [(read_children(deep, (k,), PLACE[7]), phases_of(tab7, (k,))) for k in range(4)]
    out = merge(7, blocks, even_ref, odd_ref)
    for k in range(4):
        for j in range(2):
            for half in range(2):
                cos, sin = last[k, j, half, 0], last[k, j, half, 1]
                re, im = out(k, j, 0, half), out(k, j, 1, half)
                for part, value in ((0, re * cos - im * sin), (1, re * sin + im * cos)):
                    for top in range(4):
                        base = top * 64 + (k // 2) * 32 + (k % 2) * 2 + j
                        fin[part, half, pl.ds(base, 8, stride=4), :] = value[
                            top * 8 : top * 8 + 8
                        ]
    for part in range(2):
        for half in range(2):
            o_ref[part, :, half * LANES : (half + 1) * LANES] = fin[part, half]


FAR_FIRST = (4, 3, 5, 2, 6, 1, 7)


def kernel(
    w_ref, slow_hbm, even_hbm, odd_hbm, o_ref,
    raw, swapped, relayed, packed, passing, r_ref, give, take, even_raw, odd_raw, even_ref, odd_ref, slow_ref,
    state, mid, deep, tab, tab4, tab5, tab6, tab7, last, fin,
    pair_send, pair_recv, own_sem, load_sem, ready, send, pass_recv, pass_send, recv,
    give_send, give_recv,
):
    x, y, z, core = chip()
    d = own_bits()
    xs = [along_x(x, k) for k in range(4)]
    ys = [along_y(y, k) for k in range(4)]
    zs = [along_z(z, k, core) for k in range(8)]
    plane = [(dx, dy) for dx in range(4) for dy in range(4) if (dx, dy) != (0, 0)]
    bar = pltpu.get_barrier_semaphore()

    def device(px, py, pz):
        return (px[0] + pz[0], py[0] + pz[1])

    sibling = (xs[0][0] + zs[0][0] + 1 - 2 * core, ys[0][0] + zs[0][1])

    def signal(sem, where):
        pl.semaphore_signal(sem, inc=1, device_id=where, device_id_type=MESH)

    for dz in FAR_FIRST:
        signal(bar, device(xs[0], ys[0], zs[dz]))
    signal(bar, sibling)
    for dx, dy in plane:
        signal(bar, device(xs[dx], ys[dy], zs[0]))
    mine = pltpu.make_async_copy(w_ref, raw, own_sem)
    mine.start()
    loads = [
        pltpu.make_async_copy(a, b, load_sem.at[k])
        for k, (a, b) in enumerate(
            [(slow_hbm, slow_ref), (even_hbm, even_raw), (odd_hbm, odd_raw)]
        )
    ]
    for load in loads:
        load.start()
    mine.wait()
    near_rows = [pl.multiple_of(b2 * 64 + d[4] * 32, 32) for b2 in range(2)]

    def lanes(half):
        return slice(half * LANES, (half + 1) * LANES)

    for row in near_rows:
        for to in range(2):
            for q in range(4):
                relayed[pl.ds(row * 8 + to * 4 + q, 32, stride=8), :] = raw[
                    q // 2, pl.ds(to * 128 + row, 32), lanes(q % 2)
                ]
    pl.semaphore_wait(bar, 23)
    for dx, dy in plane:
        signal(ready, device(xs[dx], ys[dy], zs[0]))
    swap = pltpu.make_async_remote_copy(
        src_ref=raw.at[:, pl.ds((1 - core) * 128, 128), :],
        dst_ref=swapped,
        send_sem=pair_send,
        recv_sem=pair_recv,
        device_id=sibling,
        device_id_type=MESH,
    )
    swap.start()

    group = 2 * d[4] + d[5]
    landing = group * 256 + tile_in_group(d) * 8
    z_place = (d[6] * 4 + d[1] * 2 + d[7]) * 8

    def tile(ref, px, py, pz):
        return ref.at[pl.ds((px[1] + py[1] + pz[2]) * 8, 8), :]

    def straight(ref, px, py, pz):
        pltpu.make_async_remote_copy(
            src_ref=tile(ref, px, py, pz),
            dst_ref=r_ref.at[pl.ds(landing, 8), :],
            send_sem=send,
            recv_sem=recv.at[group],
            device_id=device(px, py, pz),
            device_id_type=MESH,
        ).start()

    for dx in (2, 1, 3):
        spot = passing.at[pl.ds((dx - 1) * 64 + z_place, 8), :]
        for dz in FAR_FIRST:
            pltpu.make_async_remote_copy(
                src_ref=tile(relayed, xs[dx], ys[0], zs[dz]),
                dst_ref=spot,
                send_sem=send,
                recv_sem=pass_recv,
                device_id=device(xs[0], ys[0], zs[dz]),
                device_id_type=MESH,
            ).start()
        pltpu.make_async_copy(tile(relayed, xs[dx], ys[0], zs[0]), spot, pass_recv).start()
    for dz in FAR_FIRST:
        straight(relayed, xs[0], ys[0], zs[dz])
    pltpu.make_async_copy(
        tile(relayed, xs[0], ys[0], zs[0]), r_ref.at[pl.ds(landing, 8), :], recv.at[group]
    ).start()

    swap.wait()
    first_core = core == 0
    for q in range(4):
        ours = raw[q // 2, pl.ds(core * 128, 128), lanes(q % 2)]
        theirs = swapped[q // 2, :, lanes(q % 2)]
        packed[pl.ds(q, 128, stride=8), :] = jnp.where(first_core, ours, theirs)
        packed[pl.ds(4 + q, 128, stride=8), :] = jnp.where(first_core, theirs, ours)

    for load in loads:
        load.wait()
    even_ref[0:512, :], even_ref[512:1024, :] = high_low(even_raw[...])
    odd_ref[:, 0:LANES], odd_ref[:, LANES : 2 * LANES] = high_low(odd_raw[...])
    own = (
        d[0] * 8 + d[2] * 4 + d[4] * 2 + d[6],
        d[1] * 8 + d[3] * 4 + d[5] * 2 + d[7],
    )
    slow = [slow_ref[0], slow_ref[1], slow_ref[2]]
    fill_early(own, slow, tab)

    pl.semaphore_wait(ready, 15)

    def two_away(k, carry):
        px = along_x(x, 2 + k)
        for dz in (*FAR_FIRST, 0):
            straight(packed, px, ys[2], zs[dz])
        return carry

    def one_away(k, carry):
        px, py = along_x(x, 2 + lax.rem(k, 4)), along_y(y, 1 + 2 * (k // 4))
        for dz in (*FAR_FIRST, 0):
            straight(packed, px, py, zs[dz])
        return carry

    lax.fori_loop(0, 4, two_away, 0)
    lax.fori_loop(0, 8, one_away, 0)
    fill_middle(own, slow, tab4, tab5)
    pltpu.make_async_copy(passing, passing, pass_recv).wait()
    for dx in (2, 1, 3):
        for b6 in range(2):
            for b1 in range(2):
                from_row = (dx - 1) * 64 + b6 * 32 + b1 * 16
                to_row = group * 256 + (d[2] * 16 + b6 * 8 + b1 * 4 + d[3] * 2) * 8
                pltpu.make_async_remote_copy(
                    src_ref=passing.at[pl.ds(from_row, 16), :],
                    dst_ref=r_ref.at[pl.ds(to_row, 16), :],
                    send_sem=pass_send,
                    recv_sem=recv.at[group],
                    device_id=device(xs[dx], ys[0], zs[0]),
                    device_id_type=MESH,
                ).start()
    fill_late(own, slow, tab6, tab7, last)

    def arrive(g):
        block = r_ref.at[pl.ds(g * 256, 256), :]
        pltpu.make_async_copy(block, block, recv.at[g]).wait()

    def received(b4, b5, c, q):
        return r_ref[pl.ds((2 * b4 + b5) * 256 + c * 4 + q, 32, stride=8), :]

    arrive(group)
    for q in range(4):
        zero, one = received(d[4], d[5], 0, q), received(d[4], d[5], 1, q)
        take[core, q] = jnp.where(first_core, zero, one)
        give[q] = jnp.where(first_core, one, zero)
    trade = pltpu.make_async_remote_copy(
        src_ref=give,
        dst_ref=take.at[core],
        send_sem=give_send,
        recv_sem=give_recv,
        device_id=sibling,
        device_id_type=MESH,
    )
    trade.start()
    trade.wait()
    levels = (state, tab, even_ref, odd_ref)
    early_levels([(d[4], d[5])], lambda b4, b5, c, q: take[c, q], *levels)
    arrive(2 * d[4] + 1 - d[5])
    early_levels([(d[4], 1 - d[5])], received, *levels)

    def far(k, carry):
        y_from = lax.rem(y + 3 + 2 * k, 4)
        b4, b5 = lax.rem(y_from, 2), y_from // 2
        arrive(2 * b4 + b5)
        early_levels([(b4, b5)], received, *levels)
        level_four(b5, state, mid, tab4, even_ref, odd_ref)
        return carry

    lax.fori_loop(0, 2, far, 0)
    late_levels(mid, deep, tab5, tab6, tab7, last, fin, even_ref, odd_ref, o_ref)
    sent = packed.at[pl.ds(0, 992), :]
    pltpu.make_async_copy(sent, sent, send).wait()
    pltpu.make_async_copy(passing, passing, pass_send).wait()


def butterfly(weights, slowness_terms):
    hbm = pl.BlockSpec(memory_space=pltpu.HBM)
    f32, bf16 = jnp.float32, jnp.bfloat16
    return pl.pallas_call(
        kernel,
        out_shape=pltpu.VMEM((2, 256, 256), f32),
        in_specs=[hbm] * 4,
        out_specs=pl.BlockSpec(memory_space=pltpu.VMEM),
        scratch_shapes=[
            pltpu.VMEM((2, 256, 256), f32),
            pltpu.VMEM((2, 128, 256), f32),
            pltpu.VMEM((1024, LANES), f32),
            pltpu.VMEM((1024, LANES), f32),
            pltpu.VMEM((192, LANES), f32),
            pltpu.VMEM((1024, LANES), f32),
            pltpu.VMEM((4, 32, LANES), f32),
            pltpu.VMEM((2, 4, 32, LANES), f32),
            pltpu.VMEM((512, 256), f32),
            pltpu.VMEM((256, LANES), f32),
            pltpu.VMEM((1024, 256), bf16),
            pltpu.VMEM((256, 256), bf16),
            pltpu.SMEM((3,), f32),
            pltpu.VMEM((4, 2, 2, 64, LANES), f32),
            pltpu.VMEM((2, 2, 2, 2, 64, LANES), f32),
            pltpu.VMEM((4, 2, 2, 64, LANES), f32),
            pltpu.VMEM((4, 2, 2, 2, 2, 2, 32, LANES), f32),
            pltpu.VMEM((2, 2, 2, 2, 64, LANES), f32),
            pltpu.VMEM((2, 2, 2, 1, 2, 64, LANES), f32),
            pltpu.VMEM((4, 2, 2, 2, 2, 32, LANES), f32),
            pltpu.VMEM((4, 2, 2, 1, 2, 32, LANES), f32),
            pltpu.VMEM((4, 2, 2, 2, 32, LANES), f32),
            pltpu.VMEM((2, 2, 256, LANES), f32),
            pltpu.SemaphoreType.DMA,
            pltpu.SemaphoreType.DMA,
            pltpu.SemaphoreType.DMA,
            pltpu.SemaphoreType.DMA((3,)),
            pltpu.SemaphoreType.REGULAR,
            pltpu.SemaphoreType.DMA,
            pltpu.SemaphoreType.DMA,
            pltpu.SemaphoreType.DMA,
            pltpu.SemaphoreType.DMA((4,)),
            pltpu.SemaphoreType.DMA,
            pltpu.SemaphoreType.DMA,
        ],
        compiler_params=pltpu.CompilerParams(
            collective_id=0, has_side_effects=True, vmem_limit_bytes=48 * 2**20
        ),
    )(
        *(
            pltpu.with_memory_space_constraint(a, pltpu.HBM)
            for a in (
                weights,
                slowness_terms,
                jnp.asarray(even_matrix()),
                jnp.asarray(odd_matrix()),
            )
        )
    )


def local(weights, slowness_terms):
    return butterfly(weights.reshape(2, 256, 256), slowness_terms).reshape(weights.shape)


def solution(mesh):
    return jax.shard_map(
        local,
        mesh=mesh,
        in_specs=(P(None, "src", "tgt", None, None), P()),
        out_specs=P(None, "src", "tgt", None, None),
        check_vma=False,
    )
```

time: 33.6 us -> 30.7 us (0.914)
  Pallas kernels: 32.7 us -> 29.8 us
    pallas_call x1, Pallas kernels: 32.7 us -> 29.8 us  [butterfly(): pl.pallas_call(kernel, out_shape=pltpu.VMEM((2, 256, 256), f32), in_specs...]
where the time goes in v2:
time: 30.7 us; the launch traced here: 30.6 us
  Pallas kernels  29.8 us (97%)
  local copies, waits for them, and re-layouts  0.8 us (3%)
    pallas_call x1, Pallas kernels, butterfly(): pl.pallas_call(kernel, out_shape=pltpu.VMEM((2, 256, 256), f32), in_specs...  29.8 us
    unnamed x1, local copies, waits for them, and re-layouts  0.8 us

profile of v2, /device:TPU:1, one launch (start us, length us, event | category | flops | bytes accessed | tf_op | source)
XLA Modules:
  0.0 30.6 jit_solution(8136768656935156045)
XLA Ops:
  0.0 29.8 %shard_map.46 = f32[2,256,256]{2,1,0:T(8,128)S(1)} custom-call(f32[2,256,256]{2,1,0:T(8,128)} %bitcast.5, f32[3]{0:T(128)} %slow_hbm.1, f32[512,256]{1,0:T(8,128)} %constant.4.clone.even_hbm, f32[256,128]{1,0:T(8,128)} %constant.5.clone.odd_hbm), custom_call_target="tpu_custom_call" | custom-call | tf_op jit(solution)/shard_map/pallas_call | solution.py:615
  29.8 0.8 %copy.7 = f32[2,1,1,256,256]{4,3,2,1,0:T(8,128)} copy(f32[2,1,1,256,256]{4,3,2,1,0:T(8,128)S(1)} %bitcast.4) | data formatting | bytes 1048576

commit v3 on v2

--- a/solution.py
+++ b/solution.py
@@ -143,7 +143,11 @@
     return slow[2] * cos
 
 
-def level_table(n, rows, jbits, bbits, own, z, slow, store):
+def flipped(bit, role):
+    return bit + role - 2 * bit * role
+
+
+def level_table(n, rows, jbits, bbits, own, z, slow, store, bit=0):
     axis = n % 2
     done = n // 2
     width = 2.0**done / 16.0
@@ -161,7 +165,10 @@
             step_k, step_r = last[axis] - new[axis], last[2] - new[2]
         for half in range(2 if axis == 0 else 1):
             for c in range(2):
-                point = corner + width * (c + z[half])
+                child = flipped(bit, c)
+                if not isinstance(child, int):
+                    child = child.astype(jnp.float32)
+                point = corner + width * (child + z[half])
                 turns = point * step_k + shifts(point, axis, slow) * step_r
                 store(c, j, half, unit(turns))
 
@@ -248,31 +255,32 @@
     return store
 
 
-def fill_early(own, slow, tab):
+def fill_early(d, own, slow, tab):
     nodes = (lane_nodes(0, 32), lane_nodes(1, 32))
     row = lax.broadcasted_iota(jnp.int32, (32, LANES), 0)
     for n in range(4):
         index = full_index(n, row)
         jbits = {m: bit_of(index, PLACE[m]) for m in range(n)}
 
-        def one_key(key, carry, n=n, index=index, jbits=jbits):
+        def one_role(role, carry, n=n, index=index, jbits=jbits):
             bbits = {m: bit_of(index, PLACE[m]) for m in (*range(n + 1, 4), 6, 7)}
-            bbits[4] = bbits[5] = key
-            level_table(n, 32, jbits, bbits, own, nodes[n % 2], slow, keep(tab, n, key))
+            bbits[4], bbits[5] = flipped(d[4], role), flipped(d[5], role)
+            level_table(n, 32, jbits, bbits, own, nodes[n % 2], slow, keep(tab, n, role))
             return carry
 
-        lax.fori_loop(0, 2, one_key, 0)
-
-
-def fill_middle(own, slow, tab4, tab5):
+        lax.fori_loop(0, 2, one_role, 0)
+
+
+def fill_middle(d, own, slow, tab4, tab5):
     row = lax.broadcasted_iota(jnp.int32, (64, LANES), 0)
     jbits = {m: bit_of(row, PLACE[m]) for m in range(4)}
-    level_table(4, 64, jbits, {6: bit_of(row, PLACE[6])}, own, lane_nodes(0, 64), slow, keep(tab4))
+    corner = {6: bit_of(row, PLACE[6])}
+    level_table(4, 64, jbits, corner, own, lane_nodes(0, 64), slow, keep(tab4), d[4])
     nodes = lane_nodes(1, 64)
 
     def five(j4, carry):
         bbits = {7: bit_of(row, PLACE[7])}
-        level_table(5, 64, {**jbits, 4: j4}, bbits, own, nodes, slow, keep(tab5, j4))
+        level_table(5, 64, {**jbits, 4: j4}, bbits, own, nodes, slow, keep(tab5, j4), d[5])
         return carry
 
     lax.fori_loop(0, 2, five, 0)
@@ -347,28 +355,24 @@
     return lambda c, j, half: (table[(*lead, c, j, half, 0)], table[(*lead, c, j, half, 1)])
 
 
+PLACES = ((0, 0), (0, 1), (1, 1), (1, 0))
+
+
 def early_levels(groups, first, state, tab, even_ref, odd_ref):
     for n in range(4):
         blocks = []
-        for b4, b5 in groups:
-            g = 2 * b4 + b5
+        for g in groups:
             if n == 0:
                 children = [
-                    [
-                        [
-                            first(b4, b5, c, part * 2 + half)
-                            for half in range(2)
-                        ]
-                        for part in range(2)
-                    ]
+                    [[first(g, c, part * 2 + half) for half in range(2)] for part in range(2)]
                     for c in range(2)
                 ]
             else:
                 children = read_children(state, (g,), PLACE[n])
-            blocks.append((children, phases_of(tab, (n, b5 if n % 2 else b4))))
+            blocks.append((children, phases_of(tab, (n, PLACES[g][n % 2]))))
         out = merge(n, blocks, even_ref, odd_ref)
-        for at, (b4, b5) in enumerate(groups):
-            write_siblings(state, (2 * b4 + b5,), PLACE[n], out, at)
+        for at, g in enumerate(groups):
+            write_siblings(state, (g,), PLACE[n], out, at)
 
 
 QUADS = [(j, part, half) for j in range(2) for part in range(2) for half in range(2)]
@@ -380,15 +384,15 @@
     ]
 
 
-def level_four(b5, state, mid, tab4, even_ref, odd_ref):
-    out = merge(4, [(whole(state, (b5,), (2 + b5,)), phases_of(tab4, ()))], even_ref, odd_ref)
+def level_four(near, far, state, mid, tab4, even_ref, odd_ref):
+    out = merge(4, [(whole(state, (near,), (far,)), phases_of(tab4, ()))], even_ref, odd_ref)
     for j, part, half in QUADS:
-        mid[b5, j, part, half] = out(0, j, part, half)
-
-
-def late_levels(mid, deep, tab5, tab6, tab7, last, fin, even_ref, odd_ref, o_ref):
+        mid[near, j, part, half] = out(0, j, part, half)
+
+
+def late_levels(mid, deep, tab5, tab6, tab7, last, fin, even_ref, odd_ref, odd5_ref, o_ref):
     blocks = [(whole(mid, (0, j4), (1, j4)), phases_of(tab5, (j4,))) for j4 in range(2)]
-    out = merge(5, blocks, even_ref, odd_ref)
+    out = merge(5, blocks, even_ref, odd5_ref)
     for j4 in range(2):
         for j, part, half in QUADS:
             deep[2 * j4 + j, part, half] = out(j4, j, part, half)
@@ -419,7 +423,8 @@
 
 def kernel(
     w_ref, slow_hbm, even_hbm, odd_hbm, o_ref,
-    raw, swapped, relayed, packed, passing, r_ref, give, take, even_raw, odd_raw, even_ref, odd_ref, slow_ref,
+    raw, swapped, relayed, packed, passing, r_ref, give, take, even_raw, odd_raw, even_ref, odd_ref,
+    even4_ref, odd5_ref, slow_ref,
     state, mid, deep, tab, tab4, tab5, tab6, tab7, last, fin,
     pair_send, pair_recv, own_sem, load_sem, ready, send, pass_recv, pass_send, recv,
     give_send, give_recv,
@@ -480,19 +485,18 @@
     )
     swap.start()
 
-    group = 2 * d[4] + d[5]
-    landing = group * 256 + tile_in_group(d) * 8
+    place = tile_in_group(d) * 8
     z_place = (d[6] * 4 + d[1] * 2 + d[7]) * 8
 
     def tile(ref, px, py, pz):
         return ref.at[pl.ds((px[1] + py[1] + pz[2]) * 8, 8), :]
 
-    def straight(ref, px, py, pz):
+    def straight(ref, g, px, py, pz):
         pltpu.make_async_remote_copy(
             src_ref=tile(ref, px, py, pz),
-            dst_ref=r_ref.at[pl.ds(landing, 8), :],
+            dst_ref=r_ref.at[g, pl.ds(place, 8), :],
             send_sem=send,
-            recv_sem=recv.at[group],
+            recv_sem=recv.at[g],
             device_id=device(px, py, pz),
             device_id_type=MESH,
         ).start()
@@ -510,9 +514,9 @@
             ).start()
         pltpu.make_async_copy(tile(relayed, xs[dx], ys[0], zs[0]), spot, pass_recv).start()
     for dz in FAR_FIRST:
-        straight(relayed, xs[0], ys[0], zs[dz])
+        straight(relayed, 0, xs[0], ys[0], zs[dz])
     pltpu.make_async_copy(
-        tile(relayed, xs[0], ys[0], zs[0]), r_ref.at[pl.ds(landing, 8), :], recv.at[group]
+        tile(relayed, xs[0], ys[0], zs[0]), r_ref.at[0, pl.ds(place, 8), :], recv.at[0]
     ).start()
 
     swap.wait()
@@ -527,56 +531,68 @@
         load.wait()
     even_ref[0:512, :], even_ref[512:1024, :] = high_low(even_raw[...])
     odd_ref[:, 0:LANES], odd_ref[:, LANES : 2 * LANES] = high_low(odd_raw[...])
+    for c in range(2):
+        child = pl.multiple_of(flipped(d[4], c) * 256, 256)
+        high, low = high_low(even_raw[pl.ds(child, 256), :])
+        even4_ref[c * 256 : c * 256 + 256, :] = high
+        even4_ref[512 + c * 256 : 768 + c * 256, :] = low
+        child = pl.multiple_of(flipped(d[5], c) * LANES, LANES)
+        high, low = high_low(odd_raw[pl.ds(child, LANES), :])
+        odd5_ref[c * LANES : (c + 1) * LANES, 0:LANES] = high
+        odd5_ref[c * LANES : (c + 1) * LANES, LANES : 2 * LANES] = low
     own = (
         d[0] * 8 + d[2] * 4 + d[4] * 2 + d[6],
         d[1] * 8 + d[3] * 4 + d[5] * 2 + d[7],
     )
     slow = [slow_ref[0], slow_ref[1], slow_ref[2]]
-    fill_early(own, slow, tab)
 
     pl.semaphore_wait(ready, 15)
 
     def two_away(k, carry):
         px = along_x(x, 2 + k)
         for dz in (*FAR_FIRST, 0):
-            straight(packed, px, ys[2], zs[dz])
+            straight(packed, 1, px, ys[2], zs[dz])
         return carry
 
     def one_away(k, carry):
-        px, py = along_x(x, 2 + lax.rem(k, 4)), along_y(y, 1 + 2 * (k // 4))
+        px = along_x(x, 2 + lax.rem(k, 4))
+        py = along_y(y, 1 + 2 * flipped(1 - lax.rem(y, 2), k // 4))
         for dz in (*FAR_FIRST, 0):
-            straight(packed, px, py, zs[dz])
+            straight(packed, 2 + k // 4, px, py, zs[dz])
         return carry
 
     lax.fori_loop(0, 4, two_away, 0)
-    lax.fori_loop(0, 8, one_away, 0)
-    fill_middle(own, slow, tab4, tab5)
     pltpu.make_async_copy(passing, passing, pass_recv).wait()
     for dx in (2, 1, 3):
         for b6 in range(2):
             for b1 in range(2):
                 from_row = (dx - 1) * 64 + b6 * 32 + b1 * 16
-                to_row = group * 256 + (d[2] * 16 + b6 * 8 + b1 * 4 + d[3] * 2) * 8
+                to_row = (d[2] * 16 + b6 * 8 + b1 * 4 + d[3] * 2) * 8
                 pltpu.make_async_remote_copy(
                     src_ref=passing.at[pl.ds(from_row, 16), :],
-                    dst_ref=r_ref.at[pl.ds(to_row, 16), :],
+                    dst_ref=r_ref.at[0, pl.ds(to_row, 16), :],
                     send_sem=pass_send,
-                    recv_sem=recv.at[group],
+                    recv_sem=recv.at[0],
                     device_id=device(xs[dx], ys[0], zs[0]),
                     device_id_type=MESH,
                 ).start()
+    lax.fori_loop(0, 8, one_away, 0)
+    fill_early(d, own, slow, tab)
+    fill_middle(d, own, slow, tab4, tab5)
     fill_late(own, slow, tab6, tab7, last)
 
     def arrive(g):
-        block = r_ref.at[pl.ds(g * 256, 256), :]
-        pltpu.make_async_copy(block, block, recv.at[g]).wait()
-
-    def received(b4, b5, c, q):
-        return r_ref[pl.ds((2 * b4 + b5) * 256 + c * 4 + q, 32, stride=8), :]
-
-    arrive(group)
+        pltpu.make_async_copy(r_ref.at[g], r_ref.at[g], recv.at[g]).wait()
+
+    def received(g, c, q):
+        return r_ref[g, pl.ds(c * 4 + q, 32, stride=8), :]
+
+    def near(g, c, q):
+        return take[c, q] if g == 0 else received(g, c, q)
+
+    arrive(0)
     for q in range(4):
-        zero, one = received(d[4], d[5], 0, q), received(d[4], d[5], 1, q)
+        zero, one = received(0, 0, q), received(0, 1, q)
         take[core, q] = jnp.where(first_core, zero, one)
         give[q] = jnp.where(first_core, one, zero)
     trade = pltpu.make_async_remote_copy(
@@ -589,21 +605,16 @@
     )
     trade.start()
     trade.wait()
+    arrive(1)
     levels = (state, tab, even_ref, odd_ref)
-    early_levels([(d[4], d[5])], lambda b4, b5, c, q: take[c, q], *levels)
-    arrive(2 * d[4] + 1 - d[5])
-    early_levels([(d[4], 1 - d[5])], received, *levels)
-
-    def far(k, carry):
-        y_from = lax.rem(y + 3 + 2 * k, 4)
-        b4, b5 = lax.rem(y_from, 2), y_from // 2
-        arrive(2 * b4 + b5)
-        early_levels([(b4, b5)], received, *levels)
-        level_four(b5, state, mid, tab4, even_ref, odd_ref)
-        return carry
-
-    lax.fori_loop(0, 2, far, 0)
-    late_levels(mid, deep, tab5, tab6, tab7, last, fin, even_ref, odd_ref, o_ref)
+    early_levels([0, 1], near, *levels)
+    arrive(2)
+    early_levels([2], received, *levels)
+    level_four(1, 2, state, mid, tab4, even4_ref, odd_ref)
+    arrive(3)
+    early_levels([3], received, *levels)
+    level_four(0, 3, state, mid, tab4, even4_ref, odd_ref)
+    late_levels(mid, deep, tab5, tab6, tab7, last, fin, even_ref, odd_ref, odd5_ref, o_ref)
     sent = packed.at[pl.ds(0, 992), :]
     pltpu.make_async_copy(sent, sent, send).wait()
     pltpu.make_async_copy(passing, passing, pass_send).wait()
@@ -623,11 +634,13 @@
             pltpu.VMEM((1024, LANES), f32),
             pltpu.VMEM((1024, LANES), f32),
             pltpu.VMEM((192, LANES), f32),
-            pltpu.VMEM((1024, LANES), f32),
+            pltpu.VMEM((4, 256, LANES), f32),
             pltpu.VMEM((4, 32, LANES), f32),
             pltpu.VMEM((2, 4, 32, LANES), f32),
             pltpu.VMEM((512, 256), f32),
             pltpu.VMEM((256, LANES), f32),
+            pltpu.VMEM((1024, 256), bf16),
+            pltpu.VMEM((256, 256), bf16),
             pltpu.VMEM((1024, 256), bf16),
             pltpu.VMEM((256, 256), bf16),
             pltpu.SMEM((3,), f32),

time: 30.7 us -> 30.3 us (0.987)
  Pallas kernels: 29.8 us -> 29.4 us
    pallas_call x1, Pallas kernels: 29.8 us -> 29.4 us  [butterfly(): pl.pallas_call(kernel, out_shape=pltpu.VMEM((2, 256, 256), f32), in_specs...]
where the time goes in v3:
time: 30.3 us; the launch traced here: 30.2 us
  Pallas kernels  29.4 us (97%)
  local copies, waits for them, and re-layouts  0.8 us (3%)
    pallas_call x1, Pallas kernels, butterfly(): pl.pallas_call(kernel, out_shape=pltpu.VMEM((2, 256, 256), f32), in_specs...  29.4 us
    unnamed x1, local copies, waits for them, and re-layouts  0.8 us

profile of v3, /device:TPU:1, one launch (start us, length us, event | category | flops | bytes accessed | tf_op | source)
XLA Modules:
  0.0 30.2 jit_solution(9537844338941592892)
XLA Ops:
  0.0 29.4 %shard_map.46 = f32[2,256,256]{2,1,0:T(8,128)S(1)} custom-call(f32[2,256,256]{2,1,0:T(8,128)} %bitcast.5, f32[3]{0:T(128)} %slow_hbm.1, f32[512,256]{1,0:T(8,128)} %constant.4.clone.even_hbm, f32[256,128]{1,0:T(8,128)} %constant.5.clone.odd_hbm), custom_call_target="tpu_custom_call" | custom-call | tf_op jit(solution)/shard_map/pallas_call | solution.py:626
  29.4 0.8 %copy.7 = f32[2,1,1,256,256]{4,3,2,1,0:T(8,128)} copy(f32[2,1,1,256,256]{4,3,2,1,0:T(8,128)S(1)} %bitcast.4) | data formatting | bytes 1048576

commit v4 on v3

--- a/solution.py
+++ b/solution.py
@@ -206,11 +206,11 @@
         )
         count = full.shape[0]
         high, low = high_low(full)
-        both = jnp.dot(
-            jnp.concatenate([high, low]), even_ref[0:512, :], preferred_element_type=f32
+        total = jnp.dot(
+            jnp.concatenate([high, high, low], axis=1),
+            jnp.concatenate([even_ref[...], even_ref[0:512, :]]),
+            preferred_element_type=f32,
         )
-        rest = jnp.dot(high, even_ref[512:1024, :], preferred_element_type=f32)
-        total = both[:count] + (both[count:] + rest)
 
         def out(block, j, part, half):
             first = (block * 4 + 2 * j + part) * rows
@@ -445,11 +445,11 @@
     def signal(sem, where):
         pl.semaphore_signal(sem, inc=1, device_id=where, device_id_type=MESH)
 
+    for dx, dy in plane:
+        signal(bar, device(xs[dx], ys[dy], zs[0]))
     for dz in FAR_FIRST:
         signal(bar, device(xs[0], ys[0], zs[dz]))
     signal(bar, sibling)
-    for dx, dy in plane:
-        signal(bar, device(xs[dx], ys[dy], zs[0]))
     mine = pltpu.make_async_copy(w_ref, raw, own_sem)
     mine.start()
     loads = [

time: 30.3 us -> 30.3 us (level)
  no operation moved by 1% of the time
where the time goes in v4:
time: 30.3 us; the launch traced here: 30.2 us
  Pallas kernels  29.4 us (97%)
  local copies, waits for them, and re-layouts  0.8 us (3%)
    pallas_call x1, Pallas kernels, butterfly(): pl.pallas_call(kernel, out_shape=pltpu.VMEM((2, 256, 256), f32), in_specs...  29.4 us
    unnamed x1, local copies, waits for them, and re-layouts  0.8 us

profile of v4, /device:TPU:1, one launch (start us, length us, event | category | flops | bytes accessed | tf_op | source)
XLA Modules:
  0.0 30.2 jit_solution(7381703391574930365)
XLA Ops:
  0.0 29.4 %shard_map.46 = f32[2,256,256]{2,1,0:T(8,128)S(1)} custom-call(f32[2,256,256]{2,1,0:T(8,128)} %bitcast.5, f32[3]{0:T(128)} %slow_hbm.1, f32[512,256]{1,0:T(8,128)} %constant.4.clone.even_hbm, f32[256,128]{1,0:T(8,128)} %constant.5.clone.odd_hbm), custom_call_target="tpu_custom_call" | custom-call | tf_op jit(solution)/shard_map/pallas_call | solution.py:626
  29.4 0.8 %copy.7 = f32[2,1,1,256,256]{4,3,2,1,0:T(8,128)} copy(f32[2,1,1,256,256]{4,3,2,1,0:T(8,128)S(1)} %bitcast.4) | data formatting | bytes 1048576
